TPU v7x, 32 devices: a whole 2x2x4 slice. The times are simulated.
32 devices in a mesh: group: 2 (over y), query: 8 (over z, x), row: 2 (over core).
Axes of the slice: x: 2, y: 2, z: 4, core: 2. Of those that a mesh axis runs over, the one named last changes fastest.
Arguments:
- query_left: bfloat16 [64, 32, 256], P(('group', 'query'), None, 'row'), parts along dimension 0, may hold values from -2.09375 to 2.09375
- query_right: bfloat16 [64, 32, 256], P(('group', 'query')), parts along dimension 0, may hold values from -2.09375 to 2.09375
- train_left: bfloat16 [64, 32, 256], P(('group', 'query'), None, 'row'), parts along dimension 0, may hold values from -2.09375 to 2.09375
- train_right: bfloat16 [64, 32, 256], P(('group', 'query')), parts along dimension 0, may hold values from -2.09375 to 2.09375
- eigenvalues: float32 [256, 256], P('row'), may hold values from 0.05 to 5
Outputs:
- influence: float32 [64, 32], P(('group', 'query')), parts along dimension 0
There are 2 independent parts, one for each index of `group`. A program takes and returns all parts, laid end to end along the dimension named above; an argument that names none is the same for every part. Nothing has to cross between parts.
All inputs are finite; a program needn't handle non-finite values.
Results may differ from a plain program's by a relative error of at most 0.005.
Values may be sent and summed in bfloat16 or wider, within the bound.
A program may use at most 64 MiB of HBM per device.

v0:
```python
import jax
import jax.numpy as jnp
from jax import lax
from jax.sharding import PartitionSpec as P

ROWS = 256
COLS = 256


damping = 0.05


def body(query_left, query_right, train_left, train_right, eigenvalues):
    weight = 1.0 / (eigenvalues + damping)

    def condition(operands):
        query_rows, query_cols = operands
        gradient = jnp.einsum(
            "ra,rb->ab", query_rows, query_cols, preferred_element_type=jnp.float32
        )
        return (gradient * weight).astype(jnp.bfloat16)

    precond = lax.map(condition, (query_left, query_right))
    query_count, row_count, col_count = precond.shape
    flat_precond = precond.reshape(query_count * row_count, col_count)
    normalizer = float(ROWS * COLS) ** (-0.5)
    train_cols = lax.all_gather(train_right, "query", axis=0, tiled=True)
    block_count, rank_count, _ = train_cols.shape
    flat_cols = train_cols.reshape(block_count * rank_count, col_count)
    projected = lax.dot_general(
        flat_precond, flat_cols, (((1,), (1,)), ((), ())), preferred_element_type=jnp.float32
    )
    projected = projected.reshape(query_count, row_count, block_count, rank_count)
    values = (
        jnp.einsum(
            "qatr,tra->qt",
            projected,
            lax.all_gather(train_left, "query", axis=0, tiled=True).astype(jnp.float32),
        )
        * normalizer
    )
    return lax.psum(values, "row")


def solution(mesh):
    placed = (
        P(("group", "query"), None, "row"),
        P(("group", "query"), None, None),
        P(("group", "query"), None, "row"),
        P(("group", "query"), None, None),
        P("row", None),
    )
    return jax.shard_map(
        body, mesh=mesh, in_specs=placed, out_specs=P(("group", "query"), None), check_vma=False
    )
```

profile of v0, /device:TPU:0, one launch (start us, length us, event | category | flops | bytes accessed | tf_op | source)
XLA Modules:
  0.0 73.9 jit_solution(12641931854092473540)
XLA Ops:
  0.0 0.9 %add_divide_fusion = f32[128,256]{1,0:T(8,128)S(1)} fusion(f32[128,256]{1,0:T(8,128)} %param.11), kind=kLoop, calls=%fused_computation.15 | loop fusion | flops 65536 | bytes 262144 | tf_op jit(solution)/shard_map/div | solution.py:14
  0.9 0.0 copy-start
  0.9 3.8 %while.10 = (s32[]{:T(128)}, bf16[4,128,256]{2,1,0:T(8,128)(2,1)S(1)}, bf16[4,32,128]{2,1,0:T(8,128)(2,1)}, bf16[4,32,256]{2,1,0:T(8,128)(2,1)}, f32[128,256]{1,0:T(8,128)S(1)}, /*index=5*/s32[]{:T(128)}) while((s32[]{:T(128)}, bf16[4,128,256]{2,1,0:T(8,128)(2,1)S(1)}, bf16[4,32,128]{2,1,0:T(8,128)(2,1)}, bf16[4,32,256]{2,1,0:T(8,128)(2,1)}, ...), condition=%wide.region_1.2_spmd, body=%wide.region_0.1_spmd.sunk | while | flops 2162690 | bytes 222789 | solution.py:23
  1.0 1.0 %fusion.20 = bf16[4,128,256]{2,1,0:T(8,128)(2,1)S(1)} fusion(bf16[4,128,256]{2,1,0:T(8,128)(2,1)S(1)} %get-tuple-element.81, s32[]{:T(128)} %get-tuple-element.80, f32[128,256]{1,0:T(8,128)S(1)} %get-tuple-element.90, bf16[4,32,256]{2,1,0:T(8,128)(2,1)} %get-tuple-element.89, bf16[4,32,128]{2,1,0:T(8,128)(2,1)} %get-tuple-element.88), kind=kOutput, calls=%fused_computation.3.clone.1 | convolution fusion | flops 2162688 | bytes 222720 | tf_op jit(solution)/shard_map/while/body/eval_jaxpr/ra,rb->ab/dot_general | solution.py:18
  1.9 0.9 %fusion.20 = bf16[4,128,256]{2,1,0:T(8,128)(2,1)S(1)} fusion(bf16[4,128,256]{2,1,0:T(8,128)(2,1)S(1)} %get-tuple-element.81, s32[]{:T(128)} %get-tuple-element.80, f32[128,256]{1,0:T(8,128)S(1)} %get-tuple-element.90, bf16[4,32,256]{2,1,0:T(8,128)(2,1)} %get-tuple-element.89, bf16[4,32,128]{2,1,0:T(8,128)(2,1)} %get-tuple-element.88), kind=kOutput, calls=%fused_computation.3.clone.1 | convolution fusion | flops 2162688 | bytes 222720 | tf_op jit(solution)/shard_map/while/body/eval_jaxpr/ra,rb->ab/dot_general | solution.py:18
  2.9 0.9 %fusion.20 = bf16[4,128,256]{2,1,0:T(8,128)(2,1)S(1)} fusion(bf16[4,128,256]{2,1,0:T(8,128)(2,1)S(1)} %get-tuple-element.81, s32[]{:T(128)} %get-tuple-element.80, f32[128,256]{1,0:T(8,128)S(1)} %get-tuple-element.90, bf16[4,32,256]{2,1,0:T(8,128)(2,1)} %get-tuple-element.89, bf16[4,32,128]{2,1,0:T(8,128)(2,1)} %get-tuple-element.88), kind=kOutput, calls=%fused_computation.3.clone.1 | convolution fusion | flops 2162688 | bytes 222720 | tf_op jit(solution)/shard_map/while/body/eval_jaxpr/ra,rb->ab/dot_general | solution.py:18
  3.8 0.9 %fusion.20 = bf16[4,128,256]{2,1,0:T(8,128)(2,1)S(1)} fusion(bf16[4,128,256]{2,1,0:T(8,128)(2,1)S(1)} %get-tuple-element.81, s32[]{:T(128)} %get-tuple-element.80, f32[128,256]{1,0:T(8,128)S(1)} %get-tuple-element.90, bf16[4,32,256]{2,1,0:T(8,128)(2,1)} %get-tuple-element.89, bf16[4,32,128]{2,1,0:T(8,128)(2,1)} %get-tuple-element.88), kind=kOutput, calls=%fused_computation.3.clone.1 | convolution fusion | flops 2162688 | bytes 222720 | tf_op jit(solution)/shard_map/while/body/eval_jaxpr/ra,rb->ab/dot_general | solution.py:18
  4.8 0.0 copy-done
  4.8 33.0 %all_gather.6 = bf16[32,32,256]{2,1,0:T(8,128)(2,1)S(1)} all-gather(bf16[4,32,256]{2,1,0:T(8,128)(2,1)S(1)} %copy-done), channel_id=1, replica_groups=mesh['group'=2,'query'=8,'row'=2] {'query'}, dimensions={0}, use_global_device_ids=true | all-gather | bytes 589824 | tf_op jit(solution)/shard_map/all_gather | solution.py:27
  37.8 0.0 copy-start.1
  37.8 0.5 fusion.10
  38.3 0.3 copy-done.1
  38.6 30.7 %all_gather.7 = bf16[32,32,128]{2,1,0:T(8,128)(2,1)S(1)} all-gather(bf16[4,32,128]{2,1,0:T(8,128)(2,1)S(1)} %copy-done.1), channel_id=1, replica_groups=mesh['group'=2,'query'=8,'row'=2] {'query'}, dimensions={0}, use_global_device_ids=true | all-gather | bytes 294912 | tf_op jit(solution)/shard_map/all_gather | solution.py:38
  69.3 1.5 %fusion.8 = f32[32,1,4,1]{2,1,3,0:T(1,128)S(1)} fusion(bf16[4,128,32,32]{1,3,2,0:T(8,128)(2,1)S(1)} %fusion.10, bf16[32,32,128,1]{2,1,0,3:T(8,128)(2,1)S(1)} %bitcast.31), kind=kOutput, calls=%fused_computation.9 | convolution fusion | flops 1048576 | bytes 1311232 | tf_op jit(solution)/shard_map/qatr,tra->qt/dot_general | solution.py:35
  70.8 0.1 copy.9
  70.9 3.0 %psum.7 = f32[4,32]{1,0:T(4,128)} all-reduce(f32[4,32]{1,0:T(4,128)S(1)} %fusion.14), channel_id=1, replica_groups=mesh['group'=2,'query'=8,'row'=2] {'row'}, use_global_device_ids=true, to_apply=%region_2.3 | all-reduce | flops 128 | bytes 1024 | tf_op jit(solution)/shard_map/psum | solution.py:42
  (2 shorter events, 0.0 us)
Async XLA Ops:
  0.9 3.8 %copy-start = (bf16[4,32,256]{2,1,0:T(8,128)(2,1)S(1)}, bf16[4,32,256]{2,1,0:T(8,128)(2,1)}, u32[]{:S(2)}) copy-start(bf16[4,32,256]{2,1,0:T(8,128)(2,1)} %param.10) | copy-start | bytes 196612
  37.8 0.8 %copy-start.1 = (bf16[4,32,128]{2,1,0:T(8,128)(2,1)S(1)}, bf16[4,32,128]{2,1,0:T(8,128)(2,1)}, u32[]{:S(2)}) copy-start(bf16[4,32,128]{2,1,0:T(8,128)(2,1)} %param.9) | copy-start | bytes 98308
where the time goes:
time: 74.6 us; the launch traced here: 73.9 us
  blocking collectives  66.8 us (90%)
  matrix products  5.76 us (8%)
  other arithmetic  0.93 us (1%)
    all_gather x1, blocking collectives, body(): train_cols = lax.all_gather(train_right, 'query', axis=0, tiled=True)  33 us
    all_gather x1, blocking collectives, body(): lax.all_gather(train_left, 'query', axis=0, tiled=True).astype(jnp.float32)  30.7 us
    dot_general x4, matrix products, condition(): jnp.einsum('ra,rb->ab', query_rows, query_cols, preferred_element_type=jn...  3.76 us
    psum x1, blocking collectives, body(): return lax.psum(values, 'row')  3.04 us
    dot_general x1, matrix products, body(): jnp.einsum('qatr,tra->qt', projected, lax.all_gather(train_left, 'query',...  1.53 us

commit v1 on v0

v1 whole, which is shorter than its diff:
```python
import functools

import jax
import jax.numpy as jnp
from jax import lax
from jax.experimental import pallas as pl
from jax.experimental.pallas import tpu as pltpu
from jax.sharding import PartitionSpec as P

DAMPING = 0.05
MESH = pl.DeviceIdType.MESH


def each(count, step):
    if count <= 8:
        for k in range(count):
            step(k)
    else:
        lax.fori_loop(0, count, lambda k, _: (step(k), 0)[1], 0)


def kernel(
    halves,
    span,
    norm,
    ql_hbm,
    qr_hbm,
    tl_hbm,
    tr_hbm,
    eig_hbm,
    out_ref,
    ql,
    qr,
    tl,
    tr,
    eig,
    pre,
    acc,
    mine,
    parts,
    local_sem,
    q_send,
    q_recv,
    t_send,
    t_recv,
    r_send,
    r_recv,
):
    group = lax.axis_index("group")
    index = lax.axis_index("query")
    core = lax.axis_index("row")
    half = lax.div(index, span)
    place = lax.rem(index, span)
    count, rank, rows = ql_hbm.shape
    cols = qr_hbm.shape[2]

    def device(h, p, c):
        return (group, h * span + p, c)

    def place_of(d):
        return lax.bitwise_xor(place, d) if span & (span - 1) == 0 else lax.rem(place + d, span)

    def half_of(e):
        return lax.rem(half + e, halves)

    local = [
        pltpu.make_async_copy(eig_hbm, eig, local_sem.at[0]),
        pltpu.make_async_copy(ql_hbm, ql.at[half], local_sem.at[1]),
        pltpu.make_async_copy(qr_hbm, qr.at[half], local_sem.at[2]),
        pltpu.make_async_copy(tl_hbm, tl.at[place], local_sem.at[3]),
        pltpu.make_async_copy(tr_hbm, tr.at[place], local_sem.at[4]),
    ]
    for copy in local:
        copy.start()

    barrier = pltpu.get_barrier_semaphore()

    def greet(target):
        pl.semaphore_signal(barrier, inc=1, device_id=target, device_id_type=MESH)

    each(span - 1, lambda d: greet(device(half, place_of(d + 1), core)))
    for e in range(1, halves):
        for c in range(2):
            greet(device(half_of(e), place, c))
    greet(device(half, place, 1 - core))
    pl.semaphore_wait(barrier, span - 1 + 2 * (halves - 1) + 1)

    def q_copies(e, slot):
        target = device(half_of(e), place, core)
        return [
            pltpu.make_async_remote_copy(
                src, dst.at[slot], q_send.at[e, k], q_recv.at[slot, k],
                device_id=target, device_id_type=MESH,
            )
            for k, (src, dst) in enumerate([(ql_hbm, ql), (qr_hbm, qr)])
        ]

    def t_copies(d, slot):
        target = device(half, place_of(d), core)
        return [
            pltpu.make_async_remote_copy(
                src, dst.at[slot], t_send.at[d, k], t_recv.at[slot, k],
                device_id=target, device_id_type=MESH,
            )
            for k, (src, dst) in enumerate([(tr_hbm, tr), (tl_hbm, tl)])
        ]

    for e in range(1, halves):
        for copy in q_copies(e, half):
            copy.start()

    def send_t(d):
        for copy in t_copies(d + 1, place):
            copy.start()

    each(span - 1, send_t)

    local[0].wait()
    weight = jnp.transpose(1.0 / (eig[...] + DAMPING))
    local[1].wait()
    local[2].wait()

    def condition(h, position):
        for k in range(count):
            gradient = lax.dot_general(
                qr[h, k], ql[h, k], (((0,), (0,)), ((), ())), preferred_element_type=jnp.float32
            )
            start = (position * count + k) * rows
            pre[:, start : start + rows] = (gradient * weight).astype(jnp.bfloat16)

    condition(half, 0)
    for e in range(1, halves):
        slot = half_of(e)
        for copy in q_copies(e, slot):
            copy.wait_recv()
        condition(slot, e)
    local[3].wait()
    local[4].wait()
    queries = halves * count

    def score(d):
        slot = place_of(d)
        flat = tr[slot].reshape(count * rank, cols)
        left = tl[slot].astype(jnp.float32)
        for q in range(queries):
            projected = lax.dot_general(
                flat,
                pre[:, q * rows : (q + 1) * rows],
                (((1,), (0,)), ((), ())),
                preferred_element_type=jnp.float32,
            ).reshape(count, rank, rows)
            acc[slot, :, q, :] = jnp.sum(projected * left, axis=1)

    score(0)

    def score_next(d):
        for copy in t_copies(d + 1, place_of(d + 1)):
            copy.wait_recv()
        score(d + 1)

    each(span - 1, score_next)

    width = mine.shape[-1]
    lane = lax.broadcasted_iota(jnp.int32, (queries, width), 1)

    def gather(j, total):
        sums = jnp.sum(acc[j // count, j % count], axis=-1, keepdims=True)
        return jnp.where(lane == j, sums, total)

    total = jnp.zeros((queries, width), jnp.float32)
    pairs = span * count
    if pairs <= 32:
        for j in range(pairs):
            total = gather(j, total)
    else:
        total = lax.fori_loop(0, pairs, gather, total)
    total = total * norm
    for e in range(halves):
        mine[e] = total[e * count : (e + 1) * count]

    def r_copy(e, c, h, owner, k):
        return pltpu.make_async_remote_copy(
            mine.at[e], parts.at[h, owner], r_send.at[e, k], r_recv.at[h, owner],
            device_id=device(half_of(e), place, c), device_id_type=MESH,
        )

    results = []
    for e in range(1, halves):
        results.append(r_copy(e, core, half, core, 0))
        results.append(r_copy(e, 1 - core, half, core, 1))
    results.append(r_copy(0, 1 - core, half, core, 1))
    for copy in results:
        copy.start()
    parts[half, core] = mine[0]
    for e in range(1, halves):
        for c in range(2):
            r_copy(e, core, half_of(e), c, 0).wait_recv()
    r_copy(0, core, half, 1 - core, 0).wait_recv()
    out_ref[...] = jnp.concatenate(
        [(parts[h, 0] + parts[h, 1])[:, : span * count] for h in range(halves)], axis=1
    )
    for copy in results:
        copy.wait_send()
    for e in range(1, halves):
        for copy in q_copies(e, half):
            copy.wait_send()

    def sent_t(d):
        for copy in t_copies(d + 1, place):
            copy.wait_send()

    each(span - 1, sent_t)


def solution(mesh):
    n = mesh.shape["query"]
    halves = 2 if n % 2 == 0 else 1
    span = n // halves

    def body(query_left, query_right, train_left, train_right, eigenvalues):
        count, rank, rows = query_left.shape
        cols = query_right.shape[2]
        norm = float(rows * mesh.shape["row"] * cols) ** -0.5
        width = -(-span * count // 128) * 128
        bf16, f32 = jnp.bfloat16, jnp.float32
        return pl.pallas_call(
            functools.partial(kernel, halves, span, norm),
            out_shape=jax.ShapeDtypeStruct((count, n * count), f32),
            in_specs=[pl.BlockSpec(memory_space=pl.ANY)] * 5,
            out_specs=pl.BlockSpec(memory_space=pltpu.VMEM),
            scratch_shapes=[
                pltpu.VMEM((halves, count, rank, rows), bf16),
                pltpu.VMEM((halves, count, rank, cols), bf16),
                pltpu.VMEM((span, count, rank, rows), bf16),
                pltpu.VMEM((span, count, rank, cols), bf16),
                pltpu.VMEM((rows, cols), f32),
                pltpu.VMEM((cols, halves * count * rows), bf16),
                pltpu.VMEM((span, count, halves * count, rows), f32),
                pltpu.VMEM((halves, count, width), f32),
                pltpu.VMEM((halves, 2, count, width), f32),
                pltpu.SemaphoreType.DMA((5,)),
                pltpu.SemaphoreType.DMA((halves, 2)),
                pltpu.SemaphoreType.DMA((halves, 2)),
                pltpu.SemaphoreType.DMA((span, 2)),
                pltpu.SemaphoreType.DMA((span, 2)),
                pltpu.SemaphoreType.DMA((halves, 2)),
                pltpu.SemaphoreType.DMA((halves, 2)),
            ],
            compiler_params=pltpu.CompilerParams(
                collective_id=0, has_side_effects=True, vmem_limit_bytes=32 * 1024 * 1024
            ),
        )(query_left, query_right, train_left, train_right, eigenvalues)

    placed = (
        P(("group", "query"), None, "row"),
        P(("group", "query"), None, None),
        P(("group", "query"), None, "row"),
        P(("group", "query"), None, None),
        P("row", None),
    )
    return jax.shard_map(
        body, mesh=mesh, in_specs=placed, out_specs=P(("group", "query"), None), check_vma=False
    )
```

time: 74.6 us -> 22.1 us (0.30)
  blocking collectives: 66.8 us -> 0 us
  Pallas kernels: 0 us -> 17.1 us
  matrix products: 5.76 us -> 0 us
  local copies, waits for them, and re-layouts: 0.37 us -> 4.68 us
  other arithmetic: 0.93 us -> 0 us
    all_gather x2 -> x0, blocking collectives: 63.7 us -> none  [the longest x1 33 us: body(): train_cols = lax.all_gather(train_right, 'query', axis=0, tiled=True)]
    pallas_call x0 -> x1, Pallas kernels: none -> 17.1 us  [body(): pl.pallas_call(functools.partial(kernel, halves, span, norm), out_shape=j...]
    dot_general x6 -> x0, matrix products: 5.76 us -> none  [the longest x4 3.76 us: condition(): jnp.einsum('ra,rb->ab', query_rows, query_cols, preferred_element_type=jn...]
    unnamed x4 -> x11, local copies, waits for them, and re-layouts: 0.29 us -> 4.68 us
    psum x1 -> x0, blocking collectives: 3.04 us -> none  [body(): return lax.psum(values, 'row')]
    div x1 -> x0, other arithmetic: 0.93 us -> none  [body(): weight = 1.0 / (eigenvalues + damping)]
where the time goes in v1:
time: 22.1 us; the launch traced here: 21.8 us
  Pallas kernels  17.1 us (77%)
  local copies, waits for them, and re-layouts  4.68 us (21%)
    pallas_call x1, Pallas kernels, body(): pl.pallas_call(functools.partial(kernel, halves, span, norm), out_shape=j...  17.1 us
    unnamed x11, local copies, waits for them, and re-layouts  4.68 us

profile of v1, /device:TPU:0, one launch (start us, length us, event | category | flops | bytes accessed | tf_op | source)
XLA Modules:
  0.0 21.8 jit_solution(16673731943740814476)
XLA Ops:
  0.0 0.0 copy-start
  0.0 0.9 %copy-done = f32[128,256]{1,0:T(8,128)S(1)} copy-done((f32[128,256]{1,0:T(8,128)S(1)}, f32[128,256]{1,0:T(8,128)}, u32[]{:S(2)}) %copy-start) | copy-done | bytes 131096
  0.9 0.0 copy-start.1
  0.9 0.8 %copy-done.1 = bf16[4,32,256]{2,1,0:T(8,128)(2,1)S(1)} copy-done((bf16[4,32,256]{2,1,0:T(8,128)(2,1)S(1)}, bf16[4,32,256]{2,1,0:T(8,128)(2,1)}, u32[]{:S(2)}) %copy-start.1) | copy-done | bytes 65560
  1.7 0.0 copy-start.2
  1.7 0.8 %copy-done.2 = bf16[4,32,256]{2,1,0:T(8,128)(2,1)S(1)} copy-done((bf16[4,32,256]{2,1,0:T(8,128)(2,1)S(1)}, bf16[4,32,256]{2,1,0:T(8,128)(2,1)}, u32[]{:S(2)}) %copy-start.2) | copy-done | bytes 65560
  2.6 0.0 copy-start.3
  2.6 0.8 %copy-done.3 = bf16[4,32,128]{2,1,0:T(8,128)(2,1)S(1)} copy-done((bf16[4,32,128]{2,1,0:T(8,128)(2,1)S(1)}, bf16[4,32,128]{2,1,0:T(8,128)(2,1)}, u32[]{:S(2)}) %copy-start.3) | copy-done | bytes 32792
  3.3 0.0 copy-start.4
  3.3 0.8 %copy-done.4 = bf16[4,32,128]{2,1,0:T(8,128)(2,1)S(1)} copy-done((bf16[4,32,128]{2,1,0:T(8,128)(2,1)S(1)}, bf16[4,32,128]{2,1,0:T(8,128)(2,1)}, u32[]{:S(2)}) %copy-start.4) | copy-done | bytes 32792
  4.1 17.1 %shard_map.55 = f32[4,32]{1,0:T(4,128)S(1)} custom-call(bf16[4,32,128]{2,1,0:T(8,128)(2,1)S(1)} %copy-done.3, bf16[4,32,256]{2,1,0:T(8,128)(2,1)S(1)} %copy-done.1, bf16[4,32,128]{2,1,0:T(8,128)(2,1)S(1)} %copy-done.4, bf16[4,32,256]{2,1,0:T(8,128)(2,1)S(1)} %copy-done.2, f32[128,256]{1,0:T(8,128)S(1)} %copy-done), custom_call_target="tpu_custom_call" | custom-call | tf_op jit(solution)/shard_map/pallas_call | solution.py:226
  21.2 0.6 %copy.7 = f32[4,32]{1,0:T(4,128)} copy(f32[4,32]{1,0:T(4,128)S(1)} %shard_map.55) | data formatting | bytes 1024
Async XLA Ops:
  0.0 0.9 %copy-start = (f32[128,256]{1,0:T(8,128)S(1)}, f32[128,256]{1,0:T(8,128)}, u32[]{:S(2)}) copy-start(f32[128,256]{1,0:T(8,128)} %eig_hbm.1) | copy-start | bytes 393220
  0.9 0.8 %copy-start.1 = (bf16[4,32,256]{2,1,0:T(8,128)(2,1)S(1)}, bf16[4,32,256]{2,1,0:T(8,128)(2,1)}, u32[]{:S(2)}) copy-start(bf16[4,32,256]{2,1,0:T(8,128)(2,1)} %qr_hbm.1) | copy-start | bytes 196612
  1.7 0.8 %copy-start.2 = (bf16[4,32,256]{2,1,0:T(8,128)(2,1)S(1)}, bf16[4,32,256]{2,1,0:T(8,128)(2,1)}, u32[]{:S(2)}) copy-start(bf16[4,32,256]{2,1,0:T(8,128)(2,1)} %tr_hbm.1) | copy-start | bytes 196612
  2.6 0.8 %copy-start.3 = (bf16[4,32,128]{2,1,0:T(8,128)(2,1)S(1)}, bf16[4,32,128]{2,1,0:T(8,128)(2,1)}, u32[]{:S(2)}) copy-start(bf16[4,32,128]{2,1,0:T(8,128)(2,1)} %ql_hbm.1) | copy-start | bytes 98308
  3.3 0.8 %copy-start.4 = (bf16[4,32,128]{2,1,0:T(8,128)(2,1)S(1)}, bf16[4,32,128]{2,1,0:T(8,128)(2,1)}, u32[]{:S(2)}) copy-start(bf16[4,32,128]{2,1,0:T(8,128)(2,1)} %tl_hbm.1) | copy-start | bytes 98308

commit v2 on v1

--- a/solution.py
+++ b/solution.py
@@ -247,7 +247,7 @@
                 pltpu.SemaphoreType.DMA((halves, 2)),
             ],
             compiler_params=pltpu.CompilerParams(
-                collective_id=0, has_side_effects=True, vmem_limit_bytes=32 * 1024 * 1024
+                collective_id=0, has_side_effects=True, vmem_limit_bytes=60 * 1024 * 1024
             ),
         )(query_left, query_right, train_left, train_right, eigenvalues)
 

time: 22.1 us -> 18.9 us (0.86)
  local copies, waits for them, and re-layouts: 4.68 us -> 1.26 us
  Pallas kernels: 17.1 us -> 17.4 us
    unnamed x11 -> x1, local copies, waits for them, and re-layouts: 4.68 us -> 1.26 us
    pallas_call x1, Pallas kernels: 17.1 us -> 17.4 us  [body(): pl.pallas_call(functools.partial(kernel, halves, span, norm), out_shape=j...]
where the time goes in v2:
time: 18.9 us; the launch traced here: 18.7 us
  Pallas kernels  17.4 us (92%)
  local copies, waits for them, and re-layouts  1.26 us (7%)
    pallas_call x1, Pallas kernels, body(): pl.pallas_call(functools.partial(kernel, halves, span, norm), out_shape=j...  17.4 us
    unnamed x1, local copies, waits for them, and re-layouts  1.26 us

profile of v2, /device:TPU:0, one launch (start us, length us, event | category | flops | bytes accessed | tf_op | source)
XLA Modules:
  0.0 18.7 jit_solution(17702968596063130551)
XLA Ops:
  0.0 17.4 %shard_map.55 = f32[4,32]{1,0:T(4,128)} custom-call(bf16[4,32,128]{2,1,0:T(8,128)(2,1)} %ql_hbm.1, bf16[4,32,256]{2,1,0:T(8,128)(2,1)} %qr_hbm.1, bf16[4,32,128]{2,1,0:T(8,128)(2,1)} %tl_hbm.1, bf16[4,32,256]{2,1,0:T(8,128)(2,1)} %tr_hbm.1, f32[128,256]{1,0:T(8,128)} %eig_hbm.1), custom_call_target="tpu_custom_call" | custom-call | tf_op jit(solution)/shard_map/pallas_call | solution.py:226
  17.5 1.3 %copy.7 = f32[4,32]{1,0:T(4,128)} copy(f32[4,32]{1,0:T(4,128)} %shard_map.55) | data formatting | bytes 1024

commit v3 on v1

v3 whole, which is shorter than its diff:
```python
import functools

import jax
import jax.numpy as jnp
from jax import lax
from jax.experimental import pallas as pl
from jax.experimental.pallas import tpu as pltpu
from jax.sharding import PartitionSpec as P

DAMPING = 0.05
MESH = pl.DeviceIdType.MESH


def each(count, step, carry):
    if count <= 8:
        for k in range(count):
            carry = step(k, carry)
        return carry
    return lax.fori_loop(0, count, step, carry)


def kernel(
    halves,
    span,
    norm,
    ql_hbm,
    qr_hbm,
    tl_hbm,
    tr_hbm,
    eig_hbm,
    out_ref,
    ql,
    qr,
    tl,
    tr,
    eig,
    pre,
    acc,
    mine,
    parts,
    local_sem,
    s_send,
    s_recv,
    q_send,
    q_recv,
    f_send,
    f_recv,
    t_send,
    t_recv,
    r_send,
    r_recv,
):
    group = lax.axis_index("group")
    index = lax.axis_index("query")
    core = lax.axis_index("row")
    other = 1 - core
    half = lax.div(index, span)
    place = lax.rem(index, span)
    count, rank, rows = ql_hbm.shape
    cols = qr_hbm.shape[2]
    share = count // 2
    here, there = pl.ds(core * share, share), pl.ds(other * share, share)

    def place_of(d):
        return lax.bitwise_xor(place, d) if span & (span - 1) == 0 else lax.rem(place + d, span)

    def half_of(e):
        return lax.rem(half + e, halves)

    local = [
        pltpu.make_async_copy(src, dst, local_sem.at[k])
        for k, (src, dst) in enumerate(
            [
                (eig_hbm, eig.at[core]),
                (ql_hbm, ql.at[half, core]),
                (qr_hbm, qr.at[half]),
                (tl_hbm.at[here], tl.at[place, core]),
                (tr_hbm.at[here], tr.at[place]),
            ]
        )
    ]
    for copy in local:
        copy.start()

    barrier = pltpu.get_barrier_semaphore()

    def greet(h, p, c):
        pl.semaphore_signal(barrier, inc=1, device_id=(group, h * span + p, c), device_id_type=MESH)

    def greet_span(d, carry):
        greet(half, place_of(d + 1), core)
        greet(half, place_of(d + 1), other)
        return carry

    each(span - 1, greet_span, 0)
    for e in range(1, halves):
        greet(half_of(e), place, core)
        greet(half_of(e), place, other)
    greet(half, place, other)
    pl.semaphore_wait(barrier, 2 * (span - 1) + 2 * (halves - 1) + 1)

    def remote(src, dst, send, recv, h, p, c):
        return pltpu.make_async_remote_copy(
            src, dst, send, recv, device_id=(group, h * span + p, c), device_id_type=MESH
        )

    def s_copies(a):
        pairs = [
            (eig_hbm, eig.at[a]),
            (ql_hbm, ql.at[half, a]),
            (tl_hbm.at[there], tl.at[place, a]),
        ]
        return [
            remote(src, dst, s_send.at[k], s_recv.at[k], half, place, other)
            for k, (src, dst) in enumerate(pairs)
        ]

    def q_copies(e, h):
        pairs = [
            (ql_hbm, ql.at[h, core]),
            (qr_hbm.at[here], qr.at[h, here]),
        ]
        return [
            remote(src, dst, q_send.at[e, k], q_recv.at[h, k], half_of(e), place, core)
            for k, (src, dst) in enumerate(pairs)
        ]

    def f_copies(h, a, part):
        refs = [ql.at[h, a], qr.at[h, part]]
        return [
            remote(ref, ref, f_send.at[h, k], f_recv.at[h, k], half, place, other)
            for k, ref in enumerate(refs)
        ]

    def t_copies(d, p, a, b):
        target = place_of(d)
        triples = [
            (tr_hbm.at[here], tr.at[p], core),
            (tl_hbm.at[here], tl.at[p, a], core),
            (tl_hbm.at[there], tl.at[p, b], other),
        ]
        return [
            remote(src, dst, t_send.at[d, k], t_recv.at[p, k], half, target, c)
            for k, (src, dst, c) in enumerate(triples)
        ]

    for e in range(1, halves):
        for copy in q_copies(e, half):
            copy.start()
    for copy in s_copies(core):
        copy.start()

    def send_t(d, carry):
        for copy in t_copies(span - 1 - d, place, core, core):
            copy.start()
        return carry

    each(span - 1, send_t, 0)

    local[0].wait()
    local[1].wait()
    local[2].wait()
    arrivals = s_copies(other)
    arrivals[0].wait_recv()
    weight = jnp.concatenate(
        [jnp.transpose(1.0 / (eig[a] + DAMPING)) for a in range(2)], axis=1
    )
    arrivals[1].wait_recv()

    def condition(h, e):
        for k in range(count):
            gradient = lax.dot_general(
                qr[h, k],
                jnp.concatenate([ql[h, 0, k], ql[h, 1, k]], axis=1),
                (((0,), (0,)), ((), ())),
                preferred_element_type=jnp.float32,
            )
            start = (e * count + k) * 2 * rows
            pre[:, start : start + 2 * rows] = (gradient * weight).astype(jnp.bfloat16)

    width = mine.shape[-1]
    lane = lax.broadcasted_iota(jnp.int32, (count, width), 1)

    def score(d, e, total):
        slot = place_of(d)
        flat = tr[slot].reshape(share * rank, cols)
        left = [tl[slot, a].astype(jnp.float32) for a in range(2)]
        for k in range(count):
            start = (e * count + k) * 2 * rows
            projected = lax.dot_general(
                flat,
                pre[:, start : start + 2 * rows],
                (((1,), (0,)), ((), ())),
                preferred_element_type=jnp.float32,
            )
            product = (
                projected[:, :rows].reshape(share, rank, rows) * left[0]
                + projected[:, rows:].reshape(share, rank, rows) * left[1]
            )
            acc[e, :, k, :] = jnp.sum(product, axis=1)
        for t in range(share):
            sums = jnp.sum(acc[e, t], axis=-1, keepdims=True)
            total = jnp.where(lane == slot * count + core * share + t, sums, total)
        return total

    totals = [jnp.zeros((count, width), jnp.float32)] * halves
    condition(half, 0)
    local[3].wait()
    local[4].wait()
    arrivals[2].wait_recv()
    totals[0] = score(0, 0, totals[0])
    for e in range(1, halves):
        for copy in q_copies(e, half_of(e)):
            copy.wait_recv()
        for copy in f_copies(half_of(e), core, here):
            copy.start()
    for e in range(1, halves):
        for copy in f_copies(half_of(e), other, there):
            copy.wait_recv()
        condition(half_of(e), e)
        totals[e] = score(0, e, totals[e])

    def arrive(d):
        for copy in t_copies(d, place_of(d), core, other):
            copy.wait_recv()

    def score_next(d, totals):
        arrive(d + 1)
        return [score(d + 1, e, totals[e]) for e in range(halves)]

    totals = each(span - 2, score_next, totals)

    def r_copy(e, c, h, owner, k):
        return remote(mine.at[e], parts.at[h, owner], r_send.at[e, k], r_recv.at[h, owner], half_of(e), place, c)

    arrive(span - 1)
    results = []
    for e in [*range(1, halves), 0]:
        mine[e] = score(span - 1, e, totals[e]) * norm
        copies = [r_copy(e, other, half, core, 1)]
        if e:
            copies.append(r_copy(e, core, half, core, 0))
        for copy in copies:
            copy.start()
        results += copies
    parts[half, core] = mine[0]
    r_copy(0, core, half, other, 0).wait_recv()
    for e in range(1, halves):
        for c in range(2):
            r_copy(e, core, half_of(e), c, 0).wait_recv()
    out_ref[...] = jnp.concatenate(
        [(parts[h, 0] + parts[h, 1])[:, : span * count] for h in range(halves)], axis=1
    )
    for copy in results:
        copy.wait_send()
    for copy in s_copies(core):
        copy.wait_send()
    for e in range(1, halves):
        for copy in q_copies(e, half):
            copy.wait_send()
        for copy in f_copies(half_of(e), core, here):
            copy.wait_send()

    def sent_t(d, carry):
        for copy in t_copies(d + 1, place, core, core):
            copy.wait_send()
        return carry

    each(span - 1, sent_t, 0)


def solution(mesh):
    n = mesh.shape["query"]
    halves = 2 if n % 2 == 0 else 1
    span = n // halves

    def body(*operands):
        count, rank, rows = operands[0].shape
        cols = operands[1].shape[2]
        norm = float(rows * mesh.shape["row"] * cols) ** -0.5
        width = -(-span * count // 128) * 128
        bf16, f32 = jnp.bfloat16, jnp.float32
        return pl.pallas_call(
            functools.partial(kernel, halves, span, norm),
            out_shape=jax.ShapeDtypeStruct((count, n * count), f32),
            in_specs=[pl.BlockSpec(memory_space=pl.ANY)] * 5,
            out_specs=pl.BlockSpec(memory_space=pltpu.VMEM),
            scratch_shapes=[
                pltpu.VMEM((halves, 2, count, rank, rows), bf16),
                pltpu.VMEM((halves, count, rank, cols), bf16),
                pltpu.VMEM((span, 2, count // 2, rank, rows), bf16),
                pltpu.VMEM((span, count // 2, rank, cols), bf16),
                pltpu.VMEM((2, rows, cols), f32),
                pltpu.VMEM((cols, halves * count * 2 * rows), bf16),
                pltpu.VMEM((halves, count // 2, count, rows), f32),
                pltpu.VMEM((halves, count, width), f32),
                pltpu.VMEM((halves, 2, count, width), f32),
                pltpu.SemaphoreType.DMA((5,)),
                pltpu.SemaphoreType.DMA((3,)),
                pltpu.SemaphoreType.DMA((3,)),
                pltpu.SemaphoreType.DMA((halves, 2)),
                pltpu.SemaphoreType.DMA((halves, 2)),
                pltpu.SemaphoreType.DMA((halves, 2)),
                pltpu.SemaphoreType.DMA((halves, 2)),
                pltpu.SemaphoreType.DMA((span, 3)),
                pltpu.SemaphoreType.DMA((span, 3)),
                pltpu.SemaphoreType.DMA((halves, 2)),
                pltpu.SemaphoreType.DMA((halves, 2)),
            ],
            compiler_params=pltpu.CompilerParams(
                collective_id=0, has_side_effects=True, vmem_limit_bytes=32 * 1024 * 1024
            ),
        )(*(pltpu.with_memory_space_constraint(x, pltpu.HBM) for x in operands))

    placed = (
        P(("group", "query"), None, "row"),
        P(("group", "query"), None, None),
        P(("group", "query"), None, "row"),
        P(("group", "query"), None, None),
        P("row", None),
    )
    return jax.shard_map(
        body, mesh=mesh, in_specs=placed, out_specs=P(("group", "query"), None), check_vma=False
    )
```

time: 22.1 us -> 16 us (0.72)
  local copies, waits for them, and re-layouts: 4.68 us -> 0.58 us
  Pallas kernels: 17.1 us -> 15.3 us
    unnamed x11 -> x1, local copies, waits for them, and re-layouts: 4.68 us -> 0.58 us
    pallas_call x1, Pallas kernels: 17.1 us -> 15.3 us  [body(): pl.pallas_call(functools.partial(kernel, halves, span, norm), out_shape=j...]
where the time goes in v3:
time: 16 us; the launch traced here: 15.8 us
  Pallas kernels  15.3 us (96%)
  local copies, waits for them, and re-layouts  0.58 us (4%)
    pallas_call x1, Pallas kernels, body(): pl.pallas_call(functools.partial(kernel, halves, span, norm), out_shape=j...  15.3 us
    unnamed x1, local copies, waits for them, and re-layouts  0.58 us

profile of v3, /device:TPU:0, one launch (start us, length us, event | category | flops | bytes accessed | tf_op | source)
XLA Modules:
  0.0 15.8 jit_solution(9444654349785605418)
XLA Ops:
  0.0 15.3 %shard_map.55 = f32[4,32]{1,0:T(4,128)S(1)} custom-call(bf16[4,32,128]{2,1,0:T(8,128)(2,1)} %ql_hbm.1, bf16[4,32,256]{2,1,0:T(8,128)(2,1)} %qr_hbm.1, bf16[4,32,128]{2,1,0:T(8,128)(2,1)} %tl_hbm.1, bf16[4,32,256]{2,1,0:T(8,128)(2,1)} %tr_hbm.1, f32[128,256]{1,0:T(8,128)} %eig_hbm.1), custom_call_target="tpu_custom_call" | custom-call | tf_op jit(solution)/shard_map/pallas_call | solution.py:283
  15.3 0.6 %copy.7 = f32[4,32]{1,0:T(4,128)} copy(f32[4,32]{1,0:T(4,128)S(1)} %shard_map.55) | data formatting | bytes 1024

commit v4 on v3

--- a/solution.py
+++ b/solution.py
@@ -214,32 +214,24 @@
             copy.wait_recv()
         for copy in f_copies(half_of(e), core, here):
             copy.start()
+
+    def r_copy(e, c, h, owner, k):
+        return remote(mine.at[e], parts.at[h, owner], r_send.at[e, k], r_recv.at[h, owner], half_of(e), place, c)
+
+    def score_own(d, total):
+        for copy in t_copies(d + 1, place_of(d + 1), core, other):
+            copy.wait_recv()
+        return score(d + 1, 0, total)
+
+    mine[0] = each(span - 1, score_own, totals[0]) * norm
+    results = [r_copy(0, other, half, core, 1)]
+    results[0].start()
     for e in range(1, halves):
         for copy in f_copies(half_of(e), other, there):
             copy.wait_recv()
         condition(half_of(e), e)
-        totals[e] = score(0, e, totals[e])
-
-    def arrive(d):
-        for copy in t_copies(d, place_of(d), core, other):
-            copy.wait_recv()
-
-    def score_next(d, totals):
-        arrive(d + 1)
-        return [score(d + 1, e, totals[e]) for e in range(halves)]
-
-    totals = each(span - 2, score_next, totals)
-
-    def r_copy(e, c, h, owner, k):
-        return remote(mine.at[e], parts.at[h, owner], r_send.at[e, k], r_recv.at[h, owner], half_of(e), place, c)
-
-    arrive(span - 1)
-    results = []
-    for e in [*range(1, halves), 0]:
-        mine[e] = score(span - 1, e, totals[e]) * norm
-        copies = [r_copy(e, other, half, core, 1)]
-        if e:
-            copies.append(r_copy(e, core, half, core, 0))
+        mine[e] = each(span, lambda d, total: score(d, e, total), totals[e]) * norm
+        copies = [r_copy(e, other, half, core, 1), r_copy(e, core, half, core, 0)]
         for copy in copies:
             copy.start()
         results += copies

time: 16 us -> 16.7 us (1.044)
  Pallas kernels: 15.3 us -> 16 us
    pallas_call x1, Pallas kernels: 15.3 us -> 16 us  [body(): pl.pallas_call(functools.partial(kernel, halves, span, norm), out_shape=j...]
where the time goes in v4:
time: 16.7 us; the launch traced here: 16.6 us
  Pallas kernels  16 us (96%)
  local copies, waits for them, and re-layouts  0.58 us (3%)
    pallas_call x1, Pallas kernels, body(): pl.pallas_call(functools.partial(kernel, halves, span, norm), out_shape=j...  16 us
    unnamed x1, local copies, waits for them, and re-layouts  0.58 us

profile of v4, /device:TPU:0, one launch (start us, length us, event | category | flops | bytes accessed | tf_op | source)
XLA Modules:
  0.0 16.6 jit_solution(3193968018964134455)
XLA Ops:
  0.0 16.0 %shard_map.55 = f32[4,32]{1,0:T(4,128)S(1)} custom-call(bf16[4,32,128]{2,1,0:T(8,128)(2,1)} %ql_hbm.1, bf16[4,32,256]{2,1,0:T(8,128)(2,1)} %qr_hbm.1, bf16[4,32,128]{2,1,0:T(8,128)(2,1)} %tl_hbm.1, bf16[4,32,256]{2,1,0:T(8,128)(2,1)} %tr_hbm.1, f32[128,256]{1,0:T(8,128)} %eig_hbm.1), custom_call_target="tpu_custom_call" | custom-call | tf_op jit(solution)/shard_map/pallas_call | solution.py:275
  16.0 0.6 %copy.7 = f32[4,32]{1,0:T(4,128)} copy(f32[4,32]{1,0:T(4,128)S(1)} %shard_map.55) | data formatting | bytes 1024
